TPU v7x, 128 devices: a whole 4x4x4 slice. The times are simulated.
128 devices in a mesh: blk: 64 (over y, z_hi, x, core), rep: 2 (over z_lo).
Axes of the slice: x: 4, y: 4, z: 4 (z_hi: 2, z_lo: 2; z = z_hi * 2 + z_lo), core: 2. Of those that a mesh axis runs over, the one named last changes fastest.
Arguments:
- feature_codes: bfloat16 [32768, 512], P('blk', 'rep'), may hold values from -6 to 6
- group_scales: float32 [32768, 4], P('blk', 'rep'), may hold values from 0.25 to 2
- adjacency: bfloat16 [32768, 128, 128], P('blk'), may hold values from 0 to 2, as said below
- tile_source: int32 [32768], P('blk'), may hold values from 0 to 255, as said below
- tile_target: int32 [32768], P('blk'), may hold values from 0 to 3
- weight: bfloat16 [1024, 512], replicated, may hold values from -0.1875 to 0.1875
- out_bias: float32 [512], P('rep'), may hold values from -3 to 3
Outputs:
- hidden: bfloat16 [32768, 512], P('blk', 'rep')
Inputs may be any that keep to these rules, and one draw needn't show every extreme that they name: Entries 512 b to 512 (b + 1) - 1 are block b's tiles, in ascending order of tile_source; no two tiles of one block share both source and target tile. `adjacency`: entries are 0 or positive.
All inputs are finite; a program needn't handle non-finite values.
Results may differ from a plain program's by a relative error of at most 0.0052.
Values may be sent and summed in bfloat16 or wider, within the bound.
No kernel may reach another device: no remote copies, remote signals or barrier semaphores. Data moves between devices by JAX's collectives and lax.ppermute only.
A program may use at most 128 MiB of HBM per device.

v0:
```python
import functools

import jax
import jax.numpy as jnp
import numpy as np
from jax import lax
from jax.experimental import pallas as pl
from jax.experimental.pallas import tpu as pltpu
from jax.sharding import PartitionSpec as P

F = 512
TILE = 128
NTD = 4
EXTENT = (4, 2, 4, 2, 2)
VMEM_LIMIT = 8 * 2**20
TOGETHER = 16
HINT = 40


def coordinates():
    return [tuple(int(v) for v in c) for c in np.ndindex(*EXTENT)]


def linear(c):
    return int(np.ravel_multi_index(tuple(v % e for v, e in zip(c, EXTENT)), EXTENT))


class Piece:
    def __init__(self, value, tiles):
        self.value = value
        self.tiles = tiles

    def rows(self, begin, end):
        value = None if self.value is None else self.value[begin * TILE : end * TILE]
        return Piece(value, self.tiles[:, begin:end])

    def halves(self):
        count = self.tiles.shape[1]
        return self.rows(0, count // 2), self.rows(count // 2, count)


def join(*pieces):
    planned = pieces[0].value is None
    return Piece(
        None if planned else jnp.concatenate([p.value for p in pieces], axis=0),
        np.concatenate([p.tiles for p in pieces], axis=1),
    )


def moved(piece, where):
    pairs = [(linear(c), linear(where(*c))) for c in coordinates()]
    tiles = np.empty_like(piece.tiles)
    for source, target in pairs:
        tiles[target] = piece.tiles[source]
    value = piece.value
    if value is not None:
        value = lax.ppermute(value, ("blk", "rep"), pairs)
    return Piece(value, tiles)


def first_axis(piece, steps):
    return moved(
        piece,
        lambda y, h, x, c, z: (y, h, x + steps, c, z) if c == 0 else (y + steps, h, x, c, z),
    )


def second_axis(piece, steps):
    return moved(
        piece,
        lambda y, h, x, c, z: (y + steps, h, x, c, z) if c == 0 else (y, h, x + steps, c, z),
    )


def over_z(piece):
    return moved(piece, lambda y, h, x, c, z: (y, h + 1, x, c, z))


def other_core(piece):
    return moved(piece, lambda y, h, x, c, z: (y, h, x, 1 - c, z))


def after(piece, others):
    if piece.value is None:
        return piece
    return Piece(lax.optimization_barrier((piece.value, *others))[0], piece.tiles)


def plan(mine, absorb):
    plus, minus, over = (first_axis(mine, s) for s in (1, -1, 2))
    z_mine = over_z(mine)
    z_pair = over_z(join(plus, minus))
    near = join(mine, plus, minus, over, z_mine)
    near_up, near_down = second_axis(near, 1), second_axis(near, -1)
    far_up = second_axis(join(z_pair, near_up.halves()[0]), 1)
    far_down = second_axis(join(z_pair, near_down.halves()[1]), -1)
    half = NTD // 2
    at = 3 * NTD
    z_over = over_z(
        after(
            join(over, near_up.rows(at, at + half), near_down.rows(at + half, at + NTD)),
            (z_pair.value,),
        )
    )
    absorb([near, other_core(near)])
    done = absorb([near_up, near_down, other_core(near_up), other_core(near_down)])
    absorb([z_pair, other_core(z_pair)])
    end_up = join(far_up.rows(0, NTD), z_over.rows(NTD, NTD + half), z_over.rows(half, NTD))
    end_down = join(far_down.rows(NTD, 2 * NTD), z_over.rows(NTD + half, 2 * NTD), z_over.rows(0, half))
    end = join(second_axis(end_up, 1), second_axis(end_down, -1))
    absorb([far_up, far_down, z_over])
    absorb([other_core(far_up), other_core(far_down), other_core(after(z_over, (done,)))])
    absorb([end, other_core(end)], ending=True)


def start_kernel(side_ref, codes_hbm, scales_hbm, weight_hbm, features_ref, weights_ref, codes_ref, scales_ref, sems):
    rows, half = codes_ref.shape
    groups = scales_ref.shape[0]
    width = half // groups
    cols = weights_ref.shape[2]
    side = side_ref[0]
    inputs = [
        pltpu.make_async_copy(codes_hbm, codes_ref, sems.at[0]),
        pltpu.make_async_copy(scales_hbm, scales_ref, sems.at[1]),
    ]
    for n in range(4):
        whose = side if n % 2 == 0 else 1 - side
        at = pl.ds(pl.multiple_of((n // 2) * F + whose * half, half), half)
        from_here = weight_hbm.at[at, pl.ds(pl.multiple_of(side * cols, cols), cols)]
        inputs.append(pltpu.make_async_copy(from_here, weights_ref.at[n], sems.at[2 + n]))
    for copy in inputs:
        copy.start()
    for copy in inputs[:2]:
        copy.wait()
    for g in range(groups):
        at = slice(g * width, (g + 1) * width)
        scales = jnp.broadcast_to(scales_ref[g : g + 1, :], (width, rows)).T
        scaled = codes_ref[:, at].astype(jnp.float32) * scales
        features_ref[:, at] = scaled.astype(features_ref.dtype)
    for copy in inputs[2:]:
        copy.wait()


def start(side, codes, scales, weight, cols):
    rows, half = codes.shape
    there = pl.BlockSpec(memory_space=pl.ANY)
    whole = pl.BlockSpec(memory_space=pltpu.VMEM)
    scales = scales.T
    far = [pltpu.with_memory_space_constraint(x, pltpu.HBM) for x in (codes, scales, weight)]
    return pl.pallas_call(
        start_kernel,
        in_specs=[pl.BlockSpec(memory_space=pltpu.SMEM)] + [there] * 3,
        out_specs=[whole, whole],
        out_shape=[pltpu.VMEM((rows, half), codes.dtype), pltpu.VMEM((4, half, cols), weight.dtype)],
        scratch_shapes=[
            pltpu.VMEM((rows, half), codes.dtype),
            pltpu.VMEM(scales.shape, scales.dtype),
            pltpu.SemaphoreType.DMA((6,)),
        ],
        compiler_params=pltpu.CompilerParams(vmem_limit_bytes=VMEM_LIMIT),
        name="start",
    )(side[None], *far)


def mix_kernel(first, features_ref, across_ref, weights_ref, *refs):
    out_ref = refs[-1]
    mixed = jnp.dot(features_ref[...], weights_ref[first], preferred_element_type=jnp.float32)
    mixed += jnp.dot(across_ref[...], weights_ref[first + 1], preferred_element_type=jnp.float32)
    for bias_ref in refs[:-1]:
        mixed += bias_ref[...]
    out_ref[...] = mixed.astype(out_ref.dtype)


def mix(first, features, across, weights, dtype, *bias):
    whole = pl.BlockSpec(memory_space=pltpu.VMEM)
    return pl.pallas_call(
        functools.partial(mix_kernel, first),
        in_specs=[whole] * (3 + len(bias)),
        out_specs=whole,
        out_shape=pltpu.VMEM((features.shape[0], weights.shape[2]), dtype),
        compiler_params=pltpu.CompilerParams(vmem_limit_bytes=VMEM_LIMIT),
        name="mix",
    )(features, across, weights, *bias)


def load_kernel(
    parts,
    device_ref,
    spots_hbm,
    source_hbm,
    target_hbm,
    adjacency_hbm,
    tiles_ref,
    table_ref,
    spots_ref,
    source_ref,
    target_ref,
    sems,
):
    count = adjacency_hbm.shape[0]
    step = count // parts

    def copy(i):
        at = pl.ds(i * step, step)
        return pltpu.make_async_copy(adjacency_hbm.at[at], tiles_ref.at[at], sems.at[i])

    scalars = [
        pltpu.make_async_copy(spots_hbm.at[device_ref[0]], spots_ref, sems.at[parts]),
        pltpu.make_async_copy(source_hbm, source_ref, sems.at[parts + 1]),
        pltpu.make_async_copy(target_hbm, target_ref, sems.at[parts + 2]),
    ]
    for c in scalars:
        c.start()
    for i in range(parts):
        copy(i).start()
    tiles_ref[count] = jnp.zeros_like(tiles_ref[count])
    def blank(k, carry):
        table_ref[k] = count
        return carry

    lax.fori_loop(0, table_ref.shape[0], blank, 0, unroll=16)
    for c in scalars:
        c.wait()

    def add(k, carry):
        target = target_ref[k]
        source = source_ref[k]
        table_ref[spots_ref[source // TILE, source % TILE] * NTD + target] = k
        return carry

    lax.fori_loop(0, count, add, 0, unroll=8)
    for i in range(parts):
        copy(i).wait()


def degree_kernel(target_ref, tiles_ref, lanes_ref, even, odd):
    even[...] = jnp.zeros_like(even)
    odd[...] = jnp.zeros_like(odd)

    def add(k, carry):
        even[target_ref[2 * k]] += tiles_ref[2 * k].astype(jnp.float32)
        odd[target_ref[2 * k + 1]] += tiles_ref[2 * k + 1].astype(jnp.float32)
        return carry

    lax.fori_loop(0, target_ref.shape[0] // 2, add, 0, unroll=4)
    lanes_ref[...] = even[...] + odd[...]


def degree(tiles, tile_target):
    whole = pl.BlockSpec(memory_space=pltpu.VMEM)
    count = tile_target.shape[0]
    return pl.pallas_call(
        degree_kernel,
        in_specs=[pl.BlockSpec(memory_space=pltpu.SMEM), whole],
        out_specs=whole,
        out_shape=pltpu.VMEM((NTD, TILE, TILE), jnp.float32),
        scratch_shapes=[pltpu.VMEM((NTD, TILE, TILE), jnp.float32)] * 2,
        compiler_params=pltpu.CompilerParams(vmem_limit_bytes=VMEM_LIMIT),
        cost_estimate=pl.CostEstimate(
            flops=count * TILE * TILE, bytes_accessed=count * TILE * TILE * 2, transcendentals=0
        ),
        name="degree",
    )(tile_target, pltpu.with_memory_space_constraint(tiles, pltpu.VMEM))


def load(device, spots, adjacency, tile_source, tile_target):
    count = adjacency.shape[0]
    parts = 16
    there = pl.BlockSpec(memory_space=pl.ANY)
    whole = pl.BlockSpec(memory_space=pltpu.VMEM)
    scalars = pl.BlockSpec(memory_space=pltpu.SMEM)
    nodes = spots.shape[1]
    spots = jnp.asarray(spots.reshape(-1, nodes // TILE, TILE), jnp.int32)
    far = [
        pltpu.with_memory_space_constraint(x, pltpu.HBM)
        for x in (spots, tile_source, tile_target, adjacency)
    ]
    return pl.pallas_call(
        functools.partial(load_kernel, parts),
        in_specs=[scalars] + [there] * 4,
        out_specs=[whole, scalars],
        out_shape=[
            pltpu.VMEM((count + 1, TILE, TILE), adjacency.dtype),
            jax.ShapeDtypeStruct((nodes * NTD,), jnp.int32),
        ],
        scratch_shapes=[
            pltpu.SMEM((nodes // TILE, TILE), jnp.int32),
            pltpu.SMEM((count,), jnp.int32),
            pltpu.SMEM((count,), jnp.int32),
            pltpu.SemaphoreType.DMA((parts + 3,)),
        ],
        compiler_params=pltpu.CompilerParams(vmem_limit_bytes=VMEM_LIMIT),
        cost_estimate=pl.CostEstimate(
            flops=count * TILE * TILE, bytes_accessed=count * TILE * TILE * 2, transcendentals=0
        ),
        name="load",
    )(device[None], *far)


def gather_kernel(chunks, offset, first, last, table_ref, tiles_ref, *refs):
    pieces = refs[: len(chunks)]
    rest = refs[len(chunks) :]
    if last:
        total_in, lanes_ref, own_ref, out_ref, total = rest
        total[...] = total_in[...]
    elif first:
        (total,) = rest
        total[...] = jnp.zeros_like(total)
    else:
        total_in, total = rest
        total[...] = total_in[...]
    def product(piece, s, count, base):
        at = (base + s) * NTD

        def tile(t, j):
            return tiles_ref[table_ref[at + j * NTD + t]]

        left = jnp.concatenate(
            [jnp.concatenate([tile(t, j) for j in range(count)], axis=1) for t in range(NTD)],
            axis=0,
        )
        right = piece[pl.ds(pl.multiple_of(s * TILE, TILE), count * TILE)]
        return jnp.dot(left, right, preferred_element_type=jnp.float32)

    base = offset
    for piece, count in zip(pieces, chunks):

        def step(i, carry, piece=piece, base=base):
            total[...] += product(piece, i * TOGETHER, TOGETHER, base)
            return carry

        lax.fori_loop(0, count // TOGETHER, step, 0)
        if count % TOGETHER:
            total[...] += product(piece, count - count % TOGETHER, count % TOGETHER, base)
        base += count
    if last:
        degree = jnp.sum(lanes_ref[...], axis=1, keepdims=True)
        near = total[...] / jnp.sqrt(1.0 + degree)
        out_ref[...] = jnp.maximum(near + own_ref[...], 0.0).astype(out_ref.dtype)


def gathered(pieces, offset, table, tiles, width, hint, total=None, ending=None):
    tiles = pltpu.with_memory_space_constraint(tiles, pltpu.VMEM)
    chunks = [p.value.shape[0] // TILE for p in pieces]
    wide = NTD * TILE
    whole = pl.BlockSpec(memory_space=pltpu.VMEM)
    scalars = pl.BlockSpec(memory_space=pltpu.SMEM)
    extra = ([] if total is None else [total]) + ([] if ending is None else list(ending))
    count = sum(chunks)
    last = ending is not None
    return pl.pallas_call(
        functools.partial(gather_kernel, chunks, offset, total is None, last),
        in_specs=[scalars, whole] + [whole] * (len(pieces) + len(extra)),
        out_specs=whole,
        out_shape=jax.ShapeDtypeStruct((wide, width), jnp.bfloat16 if last else jnp.float32),
        scratch_shapes=[pltpu.VMEM((wide, width), jnp.float32)] if last else [],
        compiler_params=pltpu.CompilerParams(vmem_limit_bytes=VMEM_LIMIT),
        cost_estimate=pl.CostEstimate(
            flops=hint * count * TILE * wide * width,
            bytes_accessed=count * TILE * (wide + width),
            transcendentals=0,
        ),
        name="gather",
    )(table, tiles, *[p.value for p in pieces], *extra)


def body(feature_codes, group_scales, adjacency, tile_source, tile_target, weight, out_bias):
    cols = out_bias.shape[0]
    side = lax.axis_index("rep")
    device = lax.axis_index("blk") * 2 + side
    features, weights = start(side, feature_codes, group_scales, weight, cols)
    blocks = np.array([linear(c) // 2 for c in coordinates()])
    here = Piece(features, blocks[:, None] * NTD + np.arange(NTD)[None, :])
    across = moved(here, lambda y, h, x, c, z: (y, h, x, c, 1 - z))
    taken = []
    plan(Piece(None, here.tiles), lambda pieces, *_, **__: taken.extend(p.tiles for p in pieces))
    order = np.concatenate(taken, axis=1)
    spots = np.argsort(order, axis=1)
    every = np.arange(lax.axis_size("blk") * NTD)
    assert np.array_equal(np.sort(order, axis=1), np.broadcast_to(every, order.shape))
    tiles, table = load(device, spots, adjacency, tile_source, tile_target)
    near, table = lax.optimization_barrier((across.value, table))
    table, lanes = lax.optimization_barrier((table, degree(tiles, tile_target)))
    lanes = lanes.reshape(NTD * TILE, TILE)
    sent = mix(2, features, near, weights, jnp.bfloat16)
    own = mix(0, features, near, weights, jnp.float32, out_bias[None])

    total = [None]
    place = [0]

    def absorb(pieces, hint=HINT, ending=False):
        total[0] = gathered(
            pieces, place[0], table, tiles, cols, hint, total[0], (lanes, own) if ending else None
        )
        place[0] += sum(p.tiles.shape[1] for p in pieces)
        return total[0]

    plan(Piece(sent, here.tiles), absorb)
    return total[0]


def solution(mesh):
    placed = (
        P("blk", "rep"),
        P("blk", "rep"),
        P("blk", None, None),
        P("blk"),
        P("blk"),
        P(),
        P("rep"),
    )
    return jax.shard_map(
        body, mesh=mesh, in_specs=placed, out_specs=P("blk", "rep"), check_vma=False
    )
```

profile of v0, /device:TPU:1, one launch (start us, length us, event | category | flops | bytes accessed | tf_op | source)
XLA Modules:
  0.0 81.3 jit_solution(3166444341579566918)
XLA Ops:
  0.0 1.2 %start.1 = (bf16[512,256]{1,0:T(8,128)(2,1)S(1)}, bf16[4,256,256]{2,1,0:T(8,128)(2,1)S(1)}) custom-call(s32[1]{0:T(128)} %bitcast.side_ref, bf16[512,256]{1,0:T(8,128)(2,1)} %codes_hbm.1, f32[2,512]{1,0:T(2,128)} %bitcast.7, bf16[1024,512]{1,0:T(8,128)(2,1)} %weight_hbm.1), custom_call_target="tpu_custom_call" | custom-call | tf_op jit(solution)/shard_map/start/pallas_call | solution.py:150
  1.2 2.5 %collective-permute-start = (bf16[512,256]{1,0:T(8,128)(2,1)S(1)}, bf16[512,256]{1,0:T(8,128)(2,1)S(1)}, u32[]{:S(2)}, u32[]{:S(2)}) collective-permute-start(bf16[512,256]{1,0:T(8,128)(2,1)S(1)} %get-tuple-element.15.features_ref), channel_id=1, source_target_pairs={{0,1},{1,0},{2,3},{3,2},{4,5},{5,4},{6,7},{7,6},{8,9},{9,8},{10,11... | collective-permute-start | bytes 786440 | tf_op jit(solution)/shard_map/ppermute | solution.py:57
  3.8 6.6 %load.1 = (bf16[513,128,128]{2,1,0:T(8,128)(2,1)S(1)}, s32[1024]{0:T(1024)S(1)}) custom-call(s32[1]{0:T(128)} %bitcast.2.device_ref, s32[128,2,128]{2,1,0:T(2,128)} %constant.12.clone.spots_hbm, s32[512]{0:T(512)} %source_hbm.1, s32[512]{0:T(512)} %target_ref.1, bf16[512,128,128]{2,1,0:T(8,128)(2,1)} %adjacency_hbm.1), custom_call_target="tpu_custom_call" | custom-call | flops 8388608 | bytes 16777216 | tf_op jit(solution)/shard_map/load/pallas_call | solution.py:278
  10.4 0.0 collective-permute-done.across_ref
  10.4 0.3 mix.2
  10.7 1.4 %collective-permute-start.1 = (bf16[512,256]{1,0:T(8,128)(2,1)S(1)}, bf16[512,256]{1,0:T(8,128)(2,1)S(1)}, u32[]{:S(2)}, u32[]{:S(2)}) collective-permute-start(bf16[512,256]{1,0:T(8,128)(2,1)S(1)} %mix.2), channel_id=1, source_target_pairs={{0,4},{1,5},{2,34},{3,35},{4,8},{5,9},{6,38},{7,39},{8,12},{9,13},... | collective-permute-start | bytes 786440 | tf_op jit(solution)/shard_map/ppermute | solution.py:57
  12.1 1.5 %collective-permute-start.2 = (bf16[512,256]{1,0:T(8,128)(2,1)S(1)}, bf16[512,256]{1,0:T(8,128)(2,1)S(1)}, u32[]{:S(2)}, u32[]{:S(2)}) collective-permute-start(bf16[512,256]{1,0:T(8,128)(2,1)S(1)} %mix.2), channel_id=1, source_target_pairs={{0,12},{1,13},{2,98},{3,99},{4,0},{5,1},{6,102},{7,103},{8,4},{9,5... | collective-permute-start | bytes 786440 | tf_op jit(solution)/shard_map/ppermute | solution.py:57
  13.6 1.6 %collective-permute-start.4 = (bf16[512,256]{1,0:T(8,128)(2,1)S(1)}, bf16[512,256]{1,0:T(8,128)(2,1)S(1)}, u32[]{:S(2)}, u32[]{:S(2)}) collective-permute-start(bf16[512,256]{1,0:T(8,128)(2,1)S(1)} %mix.2), channel_id=1, source_target_pairs={{0,8},{1,9},{2,66},{3,67},{4,12},{5,13},{6,70},{7,71},{8,0},{9,1},... | collective-permute-start | bytes 786440 | tf_op jit(solution)/shard_map/ppermute | solution.py:57
  15.2 3.4 %collective-permute-start.5 = (bf16[512,256]{1,0:T(8,128)(2,1)S(1)}, bf16[512,256]{1,0:T(8,128)(2,1)S(1)}, u32[]{:S(2)}, u32[]{:S(2)}) collective-permute-start(bf16[512,256]{1,0:T(8,128)(2,1)S(1)} %mix.2), channel_id=1, source_target_pairs={{0,16},{1,17},{2,18},{3,19},{4,20},{5,21},{6,22},{7,23},{8,24},{9,... | collective-permute-start | bytes 786440 | tf_op jit(solution)/shard_map/ppermute | solution.py:57
  18.5 0.0 collective-permute-done.1
  18.6 0.0 copy-start
  18.6 1.1 %collective-permute-done.2 = bf16[512,256]{1,0:T(8,128)(2,1)S(1)} collective-permute-done((bf16[512,256]{1,0:T(8,128)(2,1)S(1)}, bf16[512,256]{1,0:T(8,128)(2,1)S(1)}, u32[]{:S(2)}, u32[]{:S(2)}) %collective-permute-start.2) | collective-permute-done | bytes 262176 | tf_op jit(solution)/shard_map/ppermute | solution.py:57
  19.7 1.8 %collective-permute-done.4 = bf16[512,256]{1,0:T(8,128)(2,1)S(1)} collective-permute-done((bf16[512,256]{1,0:T(8,128)(2,1)S(1)}, bf16[512,256]{1,0:T(8,128)(2,1)S(1)}, u32[]{:S(2)}, u32[]{:S(2)}) %collective-permute-start.4) | collective-permute-done | bytes 262176 | tf_op jit(solution)/shard_map/ppermute | solution.py:57
  21.6 2.0 %collective-permute-done.5 = bf16[512,256]{1,0:T(8,128)(2,1)S(1)} collective-permute-done((bf16[512,256]{1,0:T(8,128)(2,1)S(1)}, bf16[512,256]{1,0:T(8,128)(2,1)S(1)}, u32[]{:S(2)}, u32[]{:S(2)}) %collective-permute-start.5) | collective-permute-done | bytes 262176 | tf_op jit(solution)/shard_map/ppermute | solution.py:57
  23.6 2.3 %collective-permute-start.6 = (bf16[2560,256]{1,0:T(8,128)(2,1)S(1)}, bf16[2560,256]{1,0:T(8,128)(2,1)S(1)}, u32[]{:S(2)}, u32[]{:S(2)}) collective-permute-start(bf16[2560,256]{1,0:T(8,128)(2,1)S(1)} %constant_dynamic-update-slice_fusion.refs_0_), channel_id=1, source_target_pairs={{0,32},{1,33},{2,6},{3,7},{4,36},{5,37},{6,10},{7,11},{8,40},{9,41... | collective-permute-start | bytes 3932168 | tf_op jit(solution)/shard_map/ppermute | solution.py:57
  25.8 2.1 %collective-permute-start.8 = (bf16[2560,256]{1,0:T(8,128)(2,1)S(1)}, bf16[2560,256]{1,0:T(8,128)(2,1)S(1)}, u32[]{:S(2)}, u32[]{:S(2)}) collective-permute-start(bf16[2560,256]{1,0:T(8,128)(2,1)S(1)} %constant_dynamic-update-slice_fusion.refs_0_), channel_id=1, source_target_pairs={{0,96},{1,97},{2,14},{3,15},{4,100},{5,101},{6,2},{7,3},{8,104},{9... | collective-permute-start | bytes 3932168 | tf_op jit(solution)/shard_map/ppermute | solution.py:57
  27.9 1.3 %collective-permute-start.18 = (bf16[2560,256]{1,0:T(8,128)(2,1)S(1)}, bf16[2560,256]{1,0:T(8,128)(2,1)S(1)}, u32[]{:S(2)}, u32[]{:S(2)}) collective-permute-start(bf16[2560,256]{1,0:T(8,128)(2,1)S(1)} %constant_dynamic-update-slice_fusion.refs_0_), channel_id=1, source_target_pairs={{0,2},{1,3},{2,0},{3,1},{4,6},{5,7},{6,4},{7,5},{8,10},{9,11},{10,... | collective-permute-start | bytes 3932168 | tf_op jit(solution)/shard_map/ppermute | solution.py:57
  29.2 3.0 %collective-permute-start.3 = (bf16[1024,256]{1,0:T(8,128)(2,1)S(1)}, bf16[1024,256]{1,0:T(8,128)(2,1)S(1)}, u32[]{:S(2)}, u32[]{:S(2)}) collective-permute-start(bf16[1024,256]{1,0:T(8,128)(2,1)S(1)} %pad_maximum_fusion.2), channel_id=1, source_target_pairs={{0,16},{1,17},{2,18},{3,19},{4,20},{5,21},{6,22},{7,23},{8,24},{9,... | collective-permute-start | bytes 1572872 | tf_op jit(solution)/shard_map/ppermute | solution.py:57
  32.2 0.0 copy-done
  32.2 0.0 copy-start.1
  32.2 3.8 %degree.1 = f32[4,128,128]{2,1,0:T(8,128)S(1)} custom-call(s32[512]{0:T(512)S(1)} %copy-done, bf16[513,128,128]{2,1,0:T(8,128)(2,1)S(1)} %get-tuple-element.18.tiles_ref), custom_call_target="tpu_custom_call" | custom-call | flops 8388608 | bytes 16777216 | tf_op jit(solution)/shard_map/degree/pallas_call | solution.py:252
  36.0 0.0 copy-done.1
  36.0 0.3 mix.3.refs_4_
  36.3 6.8 %collective-permute-done.6.refs_0_ = bf16[2560,256]{1,0:T(8,128)(2,1)S(1)} collective-permute-done((bf16[2560,256]{1,0:T(8,128)(2,1)S(1)}, bf16[2560,256]{1,0:T(8,128)(2,1)S(1)}, u32[]{:S(2)}, u32[]{:S(2)}) %collective-permute-start.6) | collective-permute-done | bytes 1310752 | tf_op jit(solution)/shard_map/ppermute | solution.py:57
  43.1 0.0 collective-permute-done.8.refs_1_
  43.2 1.1 %collective-permute-done.3.refs_0_ = bf16[1024,256]{1,0:T(8,128)(2,1)S(1)} collective-permute-done((bf16[1024,256]{1,0:T(8,128)(2,1)S(1)}, bf16[1024,256]{1,0:T(8,128)(2,1)S(1)}, u32[]{:S(2)}, u32[]{:S(2)}) %collective-permute-start.3) | collective-permute-done | bytes 524320 | tf_op jit(solution)/shard_map/ppermute | solution.py:57
  44.3 0.2 pad_maximum_fusion
  44.5 2.6 %collective-permute-start.11 = (bf16[2304,256]{1,0:T(8,128)(2,1)S(1)}, bf16[2304,256]{1,0:T(8,128)(2,1)S(1)}, u32[]{:S(2)}, u32[]{:S(2)}) collective-permute-start(bf16[2304,256]{1,0:T(8,128)(2,1)S(1)} %get-tuple-element.25), channel_id=1, source_target_pairs={{0,96},{1,97},{2,14},{3,15},{4,100},{5,101},{6,2},{7,3},{8,104},{9... | collective-permute-start | bytes 3538952 | tf_op jit(solution)/shard_map/ppermute | solution.py:57
  47.0 0.0 collective-permute-start.7
  47.1 3.0 %collective-permute-start.9 = (bf16[1024,256]{1,0:T(8,128)(2,1)S(1)}, bf16[1024,256]{1,0:T(8,128)(2,1)S(1)}, u32[]{:S(2)}, u32[]{:S(2)}) collective-permute-start(bf16[1024,256]{1,0:T(8,128)(2,1)S(1)} %pad_maximum_fusion.3), channel_id=1, source_target_pairs={{0,16},{1,17},{2,18},{3,19},{4,20},{5,21},{6,22},{7,23},{8,24},{9,... | collective-permute-start | bytes 1572872 | tf_op jit(solution)/shard_map/ppermute | solution.py:57
  50.1 1.5 %collective-permute-start.16 = (bf16[2560,256]{1,0:T(8,128)(2,1)S(1)}, bf16[2560,256]{1,0:T(8,128)(2,1)S(1)}, u32[]{:S(2)}, u32[]{:S(2)}) collective-permute-start(bf16[2560,256]{1,0:T(8,128)(2,1)S(1)} %collective-permute-done.6.refs_0_), channel_id=1, source_target_pairs={{0,2},{1,3},{2,0},{3,1},{4,6},{5,7},{6,4},{7,5},{8,10},{9,11},{10,... | collective-permute-start | bytes 3932168 | tf_op jit(solution)/shard_map/ppermute | solution.py:57
  51.6 0.0 collective-permute-done.18.refs_1_
  51.7 0.0 collective-permute-start.17
  51.7 2.1 %gather.6.refs_4_ = f32[512,256]{1,0:T(8,128)S(1)} custom-call(s32[1024]{0:T(1024)S(1)} %get-tuple-element.19.table_ref, bf16[513,128,128]{2,1,0:T(8,128)(2,1)S(1)} %get-tuple-element.18.tiles_ref, bf16[2560,256]{1,0:T(8,128)(2,1)S(1)} %constant_dynamic-update-slice_fusion.refs_0_, bf16[2560,256]{1,0:T(8,128)(2,1)S(1)} %collective-permute-done.18.refs_1_), custom_call_target="tpu_custom_call" | custom-call | flops 26843545600 | bytes 3932160 | tf_op jit(solution)/shard_map/gather/pallas_call | solution.py:351
  53.8 7.1 %collective-permute-done.9.refs_2_ = bf16[1024,256]{1,0:T(8,128)(2,1)S(1)} collective-permute-done((bf16[1024,256]{1,0:T(8,128)(2,1)S(1)}, bf16[1024,256]{1,0:T(8,128)(2,1)S(1)}, u32[]{:S(2)}, u32[]{:S(2)}) %collective-permute-start.9) | collective-permute-done | bytes 524320 | tf_op jit(solution)/shard_map/ppermute | solution.py:57
  60.9 2.1 %collective-permute-start.20 = (bf16[1024,256]{1,0:T(8,128)(2,1)S(1)}, bf16[1024,256]{1,0:T(8,128)(2,1)S(1)}, u32[]{:S(2)}, u32[]{:S(2)}) collective-permute-start(bf16[1024,256]{1,0:T(8,128)(2,1)S(1)} %collective-permute-done.3.refs_0_), channel_id=1, source_target_pairs={{0,2},{1,3},{2,0},{3,1},{4,6},{5,7},{6,4},{7,5},{8,10},{9,11},{10,... | collective-permute-start | bytes 1572872 | tf_op jit(solution)/shard_map/ppermute | solution.py:57
  63.1 0.0 collective-permute-done.11.refs_1_
  63.1 2.7 %collective-permute-start.12 = (bf16[1024,256]{1,0:T(8,128)(2,1)S(1)}, bf16[1024,256]{1,0:T(8,128)(2,1)S(1)}, u32[]{:S(2)}, u32[]{:S(2)}) collective-permute-start(bf16[1024,256]{1,0:T(8,128)(2,1)S(1)} %pad_maximum_fusion.5), channel_id=1, source_target_pairs={{0,96},{1,97},{2,14},{3,15},{4,100},{5,101},{6,2},{7,3},{8,104},{9... | collective-permute-start | bytes 1572872 | tf_op jit(solution)/shard_map/ppermute | solution.py:57
  65.9 0.0 collective-permute-done.7.refs_0_
  66.0 0.1 collective-permute-start.10
  66.0 0.0 collective-permute-done.16.refs_2_
  66.0 0.1 collective-permute-start.14
  66.1 0.0 collective-permute-done.17.refs_3_
  66.2 0.5 collective-permute-start.15
  66.6 3.5 %gather.7.refs_2_ = f32[512,256]{1,0:T(8,128)S(1)} custom-call(s32[1024]{0:T(1024)S(1)} %get-tuple-element.19.table_ref, bf16[513,128,128]{2,1,0:T(8,128)(2,1)S(1)} %get-tuple-element.18.tiles_ref, bf16[2560,256]{1,0:T(8,128)(2,1)S(1)} %collective-permute-done.6.refs_0_, bf16[2560,256]{1,0:T(8,128)(2,1)S(1)} %collective-permute-done.8.refs_1_, ...), custom_call_target="tpu_custom_call" | custom-call | flops 53687091200 | bytes 7864320 | tf_op jit(solution)/shard_map/gather/pallas_call | solution.py:351
  70.1 0.0 collective-permute-done.20.refs_1_
  70.1 0.4 collective-permute-start.19
  70.5 1.3 %gather.8.refs_3_ = f32[512,256]{1,0:T(8,128)S(1)} custom-call(s32[1024]{0:T(1024)S(1)} %get-tuple-element.19.table_ref, bf16[513,128,128]{2,1,0:T(8,128)(2,1)S(1)} %get-tuple-element.18.tiles_ref, bf16[1024,256]{1,0:T(8,128)(2,1)S(1)} %collective-permute-done.3.refs_0_, bf16[1024,256]{1,0:T(8,128)(2,1)S(1)} %collective-permute-done.20.refs_1_, ...), custom_call_target="tpu_custom_call" | custom-call | flops 10737418240 | bytes 1572864 | tf_op jit(solution)/shard_map/gather/pallas_call | solution.py:351
  71.8 2.2 %gather.9.refs_3_ = f32[512,256]{1,0:T(8,128)S(1)} custom-call(s32[1024]{0:T(1024)S(1)} %get-tuple-element.19.table_ref, bf16[513,128,128]{2,1,0:T(8,128)(2,1)S(1)} %get-tuple-element.18.tiles_ref, bf16[2304,256]{1,0:T(8,128)(2,1)S(1)} %collective-permute-done.7.refs_0_, bf16[2304,256]{1,0:T(8,128)(2,1)S(1)} %collective-permute-done.11.refs_1_, ...), custom_call_target="tpu_custom_call" | custom-call | flops 29527900160 | bytes 4325376 | tf_op jit(solution)/shard_map/gather/pallas_call | solution.py:351
  74.0 1.5 %collective-permute-done.10 = bf16[1024,256]{1,0:T(8,128)(2,1)S(1)} collective-permute-done((bf16[1024,256]{1,0:T(8,128)(2,1)S(1)}, bf16[1024,256]{1,0:T(8,128)(2,1)S(1)}, u32[]{:S(2)}, u32[]{:S(2)}) %collective-permute-start.10) | collective-permute-done | bytes 524320 | tf_op jit(solution)/shard_map/ppermute | solution.py:57
  75.6 0.0 collective-permute-done.12
  75.7 0.8 %collective-permute-start.13 = (bf16[2048,256]{1,0:T(8,128)(2,1)S(1)}, bf16[2048,256]{1,0:T(8,128)(2,1)S(1)}, u32[]{:S(2)}, u32[]{:S(2)}) collective-permute-start(bf16[2048,256]{1,0:T(8,128)(2,1)S(1)} %constant_dynamic-update-slice_fusion.5.refs_0_), channel_id=1, source_target_pairs={{0,2},{1,3},{2,0},{3,1},{4,6},{5,7},{6,4},{7,5},{8,10},{9,11},{10,... | collective-permute-start | bytes 3145736 | tf_op jit(solution)/shard_map/ppermute | solution.py:57
  76.5 0.0 collective-permute-done.19.refs_2_
  76.5 0.0 collective-permute-done.14.refs_0_
  76.5 0.0 collective-permute-done.15.refs_1_
  76.5 2.2 %gather.10.refs_2_ = f32[512,256]{1,0:T(8,128)S(1)} custom-call(s32[1024]{0:T(1024)S(1)} %get-tuple-element.19.table_ref, bf16[513,128,128]{2,1,0:T(8,128)(2,1)S(1)} %get-tuple-element.18.tiles_ref, bf16[2304,256]{1,0:T(8,128)(2,1)S(1)} %collective-permute-done.14.refs_0_, bf16[2304,256]{1,0:T(8,128)(2,1)S(1)} %collective-permute-done.15.refs_1_, ...), custom_call_target="tpu_custom_call" | custom-call | flops 29527900160 | bytes 4325376 | tf_op jit(solution)/shard_map/gather/pallas_call | solution.py:351
  78.8 0.0 collective-permute-done.13.refs_1_
  78.8 2.6 %gather.11 = bf16[512,256]{1,0:T(8,128)(2,1)} custom-call(s32[1024]{0:T(1024)S(1)} %get-tuple-element.19.table_ref, bf16[513,128,128]{2,1,0:T(8,128)(2,1)S(1)} %get-tuple-element.18.tiles_ref, bf16[2048,256]{1,0:T(8,128)(2,1)S(1)} %constant_dynamic-update-slice_fusion.5.refs_0_, bf16[2048,256]{1,0:T(8,128)(2,1)S(1)} %collective-permute-done.13.refs_1_, ...), custom_call_target="tpu_custom_call" | custom-call | flops 21474836480 | bytes 3145728 | tf_op jit(solution)/shard_map/gather/pallas_call | solution.py:351
  (18 shorter events, 0.5 us)
Async XLA Ops:
  1.2 9.2 %collective-permute-start = (bf16[512,256]{1,0:T(8,128)(2,1)S(1)}, bf16[512,256]{1,0:T(8,128)(2,1)S(1)}, u32[]{:S(2)}, u32[]{:S(2)}) collective-permute-start(bf16[512,256]{1,0:T(8,128)(2,1)S(1)} %get-tuple-element.15.features_ref), channel_id=1, source_target_pairs={{0,1},{1,0},{2,3},{3,2},{4,5},{5,4},{6,7},{7,6},{8,9},{9,8},{10,11... | collective-permute-start | bytes 786440 | tf_op jit(solution)/shard_map/ppermute | solution.py:57
  10.7 7.8 %collective-permute-start.1 = (bf16[512,256]{1,0:T(8,128)(2,1)S(1)}, bf16[512,256]{1,0:T(8,128)(2,1)S(1)}, u32[]{:S(2)}, u32[]{:S(2)}) collective-permute-start(bf16[512,256]{1,0:T(8,128)(2,1)S(1)} %mix.2), channel_id=1, source_target_pairs={{0,4},{1,5},{2,34},{3,35},{4,8},{5,9},{6,38},{7,39},{8,12},{9,13},... | collective-permute-start | bytes 786440 | tf_op jit(solution)/shard_map/ppermute | solution.py:57
  12.1 7.6 %collective-permute-start.2 = (bf16[512,256]{1,0:T(8,128)(2,1)S(1)}, bf16[512,256]{1,0:T(8,128)(2,1)S(1)}, u32[]{:S(2)}, u32[]{:S(2)}) collective-permute-start(bf16[512,256]{1,0:T(8,128)(2,1)S(1)} %mix.2), channel_id=1, source_target_pairs={{0,12},{1,13},{2,98},{3,99},{4,0},{5,1},{6,102},{7,103},{8,4},{9,5... | collective-permute-start | bytes 786440 | tf_op jit(solution)/shard_map/ppermute | solution.py:57
  13.6 8.0 %collective-permute-start.4 = (bf16[512,256]{1,0:T(8,128)(2,1)S(1)}, bf16[512,256]{1,0:T(8,128)(2,1)S(1)}, u32[]{:S(2)}, u32[]{:S(2)}) collective-permute-start(bf16[512,256]{1,0:T(8,128)(2,1)S(1)} %mix.2), channel_id=1, source_target_pairs={{0,8},{1,9},{2,66},{3,67},{4,12},{5,13},{6,70},{7,71},{8,0},{9,1},... | collective-permute-start | bytes 786440 | tf_op jit(solution)/shard_map/ppermute | solution.py:57
  15.2 8.4 %collective-permute-start.5 = (bf16[512,256]{1,0:T(8,128)(2,1)S(1)}, bf16[512,256]{1,0:T(8,128)(2,1)S(1)}, u32[]{:S(2)}, u32[]{:S(2)}) collective-permute-start(bf16[512,256]{1,0:T(8,128)(2,1)S(1)} %mix.2), channel_id=1, source_target_pairs={{0,16},{1,17},{2,18},{3,19},{4,20},{5,21},{6,22},{7,23},{8,24},{9,... | collective-permute-start | bytes 786440 | tf_op jit(solution)/shard_map/ppermute | solution.py:57
  18.6 13.6 %copy-start = (s32[512]{0:T(512)S(1)}, s32[512]{0:T(512)}, u32[]{:S(2)}) copy-start(s32[512]{0:T(512)} %target_ref.1) | copy-start | bytes 6148
  23.6 19.5 %collective-permute-start.6 = (bf16[2560,256]{1,0:T(8,128)(2,1)S(1)}, bf16[2560,256]{1,0:T(8,128)(2,1)S(1)}, u32[]{:S(2)}, u32[]{:S(2)}) collective-permute-start(bf16[2560,256]{1,0:T(8,128)(2,1)S(1)} %constant_dynamic-update-slice_fusion.refs_0_), channel_id=1, source_target_pairs={{0,32},{1,33},{2,6},{3,7},{4,36},{5,37},{6,10},{7,11},{8,40},{9,41... | collective-permute-start | bytes 3932168 | tf_op jit(solution)/shard_map/ppermute | solution.py:57
  25.8 17.3 %collective-permute-start.8 = (bf16[2560,256]{1,0:T(8,128)(2,1)S(1)}, bf16[2560,256]{1,0:T(8,128)(2,1)S(1)}, u32[]{:S(2)}, u32[]{:S(2)}) collective-permute-start(bf16[2560,256]{1,0:T(8,128)(2,1)S(1)} %constant_dynamic-update-slice_fusion.refs_0_), channel_id=1, source_target_pairs={{0,96},{1,97},{2,14},{3,15},{4,100},{5,101},{6,2},{7,3},{8,104},{9... | collective-permute-start | bytes 3932168 | tf_op jit(solution)/shard_map/ppermute | solution.py:57
  27.9 23.8 %collective-permute-start.18 = (bf16[2560,256]{1,0:T(8,128)(2,1)S(1)}, bf16[2560,256]{1,0:T(8,128)(2,1)S(1)}, u32[]{:S(2)}, u32[]{:S(2)}) collective-permute-start(bf16[2560,256]{1,0:T(8,128)(2,1)S(1)} %constant_dynamic-update-slice_fusion.refs_0_), channel_id=1, source_target_pairs={{0,2},{1,3},{2,0},{3,1},{4,6},{5,7},{6,4},{7,5},{8,10},{9,11},{10,... | collective-permute-start | bytes 3932168 | tf_op jit(solution)/shard_map/ppermute | solution.py:57
  29.2 15.1 %collective-permute-start.3 = (bf16[1024,256]{1,0:T(8,128)(2,1)S(1)}, bf16[1024,256]{1,0:T(8,128)(2,1)S(1)}, u32[]{:S(2)}, u32[]{:S(2)}) collective-permute-start(bf16[1024,256]{1,0:T(8,128)(2,1)S(1)} %pad_maximum_fusion.2), channel_id=1, source_target_pairs={{0,16},{1,17},{2,18},{3,19},{4,20},{5,21},{6,22},{7,23},{8,24},{9,... | collective-permute-start | bytes 1572872 | tf_op jit(solution)/shard_map/ppermute | solution.py:57
  32.2 3.8 %copy-start.1 = (f32[256]{0:T(256)S(1)}, f32[256]{0:T(256)}, u32[]{:S(2)}) copy-start(f32[256]{0:T(256)} %param.14) | copy-start | bytes 3076
  44.5 18.6 %collective-permute-start.11 = (bf16[2304,256]{1,0:T(8,128)(2,1)S(1)}, bf16[2304,256]{1,0:T(8,128)(2,1)S(1)}, u32[]{:S(2)}, u32[]{:S(2)}) collective-permute-start(bf16[2304,256]{1,0:T(8,128)(2,1)S(1)} %get-tuple-element.25), channel_id=1, source_target_pairs={{0,96},{1,97},{2,14},{3,15},{4,100},{5,101},{6,2},{7,3},{8,104},{9... | collective-permute-start | bytes 3538952 | tf_op jit(solution)/shard_map/ppermute | solution.py:57
  47.0 18.9 %collective-permute-start.7 = (bf16[2304,256]{1,0:T(8,128)(2,1)S(1)}, bf16[2304,256]{1,0:T(8,128)(2,1)S(1)}, u32[]{:S(2)}, u32[]{:S(2)}) collective-permute-start(bf16[2304,256]{1,0:T(8,128)(2,1)S(1)} %get-tuple-element.26), channel_id=1, source_target_pairs={{0,32},{1,33},{2,6},{3,7},{4,36},{5,37},{6,10},{7,11},{8,40},{9,41... | collective-permute-start | bytes 3538952 | tf_op jit(solution)/shard_map/ppermute | solution.py:57
  47.1 13.8 %collective-permute-start.9 = (bf16[1024,256]{1,0:T(8,128)(2,1)S(1)}, bf16[1024,256]{1,0:T(8,128)(2,1)S(1)}, u32[]{:S(2)}, u32[]{:S(2)}) collective-permute-start(bf16[1024,256]{1,0:T(8,128)(2,1)S(1)} %pad_maximum_fusion.3), channel_id=1, source_target_pairs={{0,16},{1,17},{2,18},{3,19},{4,20},{5,21},{6,22},{7,23},{8,24},{9,... | collective-permute-start | bytes 1572872 | tf_op jit(solution)/shard_map/ppermute | solution.py:57
  50.1 15.9 %collective-permute-start.16 = (bf16[2560,256]{1,0:T(8,128)(2,1)S(1)}, bf16[2560,256]{1,0:T(8,128)(2,1)S(1)}, u32[]{:S(2)}, u32[]{:S(2)}) collective-permute-start(bf16[2560,256]{1,0:T(8,128)(2,1)S(1)} %collective-permute-done.6.refs_0_), channel_id=1, source_target_pairs={{0,2},{1,3},{2,0},{3,1},{4,6},{5,7},{6,4},{7,5},{8,10},{9,11},{10,... | collective-permute-start | bytes 3932168 | tf_op jit(solution)/shard_map/ppermute | solution.py:57
  51.7 14.5 %collective-permute-start.17 = (bf16[2560,256]{1,0:T(8,128)(2,1)S(1)}, bf16[2560,256]{1,0:T(8,128)(2,1)S(1)}, u32[]{:S(2)}, u32[]{:S(2)}) collective-permute-start(bf16[2560,256]{1,0:T(8,128)(2,1)S(1)} %collective-permute-done.8.refs_1_), channel_id=1, source_target_pairs={{0,2},{1,3},{2,0},{3,1},{4,6},{5,7},{6,4},{7,5},{8,10},{9,11},{10,... | collective-permute-start | bytes 3932168 | tf_op jit(solution)/shard_map/ppermute | solution.py:57
  60.9 9.2 %collective-permute-start.20 = (bf16[1024,256]{1,0:T(8,128)(2,1)S(1)}, bf16[1024,256]{1,0:T(8,128)(2,1)S(1)}, u32[]{:S(2)}, u32[]{:S(2)}) collective-permute-start(bf16[1024,256]{1,0:T(8,128)(2,1)S(1)} %collective-permute-done.3.refs_0_), channel_id=1, source_target_pairs={{0,2},{1,3},{2,0},{3,1},{4,6},{5,7},{6,4},{7,5},{8,10},{9,11},{10,... | collective-permute-start | bytes 1572872 | tf_op jit(solution)/shard_map/ppermute | solution.py:57
  63.1 12.5 %collective-permute-start.12 = (bf16[1024,256]{1,0:T(8,128)(2,1)S(1)}, bf16[1024,256]{1,0:T(8,128)(2,1)S(1)}, u32[]{:S(2)}, u32[]{:S(2)}) collective-permute-start(bf16[1024,256]{1,0:T(8,128)(2,1)S(1)} %pad_maximum_fusion.5), channel_id=1, source_target_pairs={{0,96},{1,97},{2,14},{3,15},{4,100},{5,101},{6,2},{7,3},{8,104},{9... | collective-permute-start | bytes 1572872 | tf_op jit(solution)/shard_map/ppermute | solution.py:57
  66.0 9.6 %collective-permute-start.10 = (bf16[1024,256]{1,0:T(8,128)(2,1)S(1)}, bf16[1024,256]{1,0:T(8,128)(2,1)S(1)}, u32[]{:S(2)}, u32[]{:S(2)}) collective-permute-start(bf16[1024,256]{1,0:T(8,128)(2,1)S(1)} %pad_maximum_fusion.4), channel_id=1, source_target_pairs={{0,32},{1,33},{2,6},{3,7},{4,36},{5,37},{6,10},{7,11},{8,40},{9,41... | collective-permute-start | bytes 1572872 | tf_op jit(solution)/shard_map/ppermute | solution.py:57
  66.0 10.5 %collective-permute-start.14 = (bf16[2304,256]{1,0:T(8,128)(2,1)S(1)}, bf16[2304,256]{1,0:T(8,128)(2,1)S(1)}, u32[]{:S(2)}, u32[]{:S(2)}) collective-permute-start(bf16[2304,256]{1,0:T(8,128)(2,1)S(1)} %collective-permute-done.7.refs_0_), channel_id=1, source_target_pairs={{0,2},{1,3},{2,0},{3,1},{4,6},{5,7},{6,4},{7,5},{8,10},{9,11},{10,... | collective-permute-start | bytes 3538952 | tf_op jit(solution)/shard_map/ppermute | solution.py:57
  66.2 10.4 %collective-permute-start.15 = (bf16[2304,256]{1,0:T(8,128)(2,1)S(1)}, bf16[2304,256]{1,0:T(8,128)(2,1)S(1)}, u32[]{:S(2)}, u32[]{:S(2)}) collective-permute-start(bf16[2304,256]{1,0:T(8,128)(2,1)S(1)} %collective-permute-done.11.refs_1_), channel_id=1, source_target_pairs={{0,2},{1,3},{2,0},{3,1},{4,6},{5,7},{6,4},{7,5},{8,10},{9,11},{10,... | collective-permute-start | bytes 3538952 | tf_op jit(solution)/shard_map/ppermute | solution.py:57
  70.1 6.4 %collective-permute-start.19 = (bf16[1024,256]{1,0:T(8,128)(2,1)S(1)}, bf16[1024,256]{1,0:T(8,128)(2,1)S(1)}, u32[]{:S(2)}, u32[]{:S(2)}) collective-permute-start(bf16[1024,256]{1,0:T(8,128)(2,1)S(1)} %collective-permute-done.9.refs_2_), channel_id=1, source_target_pairs={{0,2},{1,3},{2,0},{3,1},{4,6},{5,7},{6,4},{7,5},{8,10},{9,11},{10,... | collective-permute-start | bytes 1572872 | tf_op jit(solution)/shard_map/ppermute | solution.py:57
  75.7 3.1 %collective-permute-start.13 = (bf16[2048,256]{1,0:T(8,128)(2,1)S(1)}, bf16[2048,256]{1,0:T(8,128)(2,1)S(1)}, u32[]{:S(2)}, u32[]{:S(2)}) collective-permute-start(bf16[2048,256]{1,0:T(8,128)(2,1)S(1)} %constant_dynamic-update-slice_fusion.5.refs_0_), channel_id=1, source_target_pairs={{0,2},{1,3},{2,0},{3,1},{4,6},{5,7},{6,4},{7,5},{8,10},{9,11},{10,... | collective-permute-start | bytes 3145736 | tf_op jit(solution)/shard_map/ppermute | solution.py:57
where the time goes:
time: 81.5 us; the launch traced here: 81.3 us
  starting transfers between devices  32.8 us (40%)
  Pallas kernels  26.1 us (32%)
  waiting for transfers between devices  21.4 us (26%)
    ppermute x21, starting transfers between devices, moved(): value = lax.ppermute(value, ('blk', 'rep'), pairs)  32.8 us
    ppermute x21, waiting for transfers between devices, moved(): value = lax.ppermute(value, ('blk', 'rep'), pairs)  21.4 us
    pallas_call x6, Pallas kernels, gathered(): pl.pallas_call(functools.partial(gather_kernel, chunks, offset, total is...  13.9 us
    pallas_call x1, Pallas kernels, load(): pl.pallas_call(functools.partial(load_kernel, parts), in_specs=[scalars]...  6.61 us
    pallas_call x1, Pallas kernels, degree(): pl.pallas_call(degree_kernel, in_specs=[pl.BlockSpec(memory_space=pltpu.S...  3.79 us
  transfers between devices with their start and end apart: 21, of which 7 were waited for; matrix products, arithmetic and copies ran while one was open for 1% of the time, Pallas kernels for 27%

commit v1 on v0

--- a/solution.py
+++ b/solution.py
@@ -92,8 +92,8 @@
     z_pair = over_z(join(plus, minus))
     near = join(mine, plus, minus, over, z_mine)
     near_up, near_down = second_axis(near, 1), second_axis(near, -1)
-    far_up = second_axis(join(z_pair, near_up.halves()[0]), 1)
-    far_down = second_axis(join(z_pair, near_down.halves()[1]), -1)
+    far_up = second_axis(join(z_pair, near_up.rows(0, 9)), 1)
+    far_down = second_axis(join(z_pair, near_down.rows(9, 20)), -1)
     half = NTD // 2
     at = 3 * NTD
     z_over = over_z(

time: 81.5 us -> 80.5 us (0.988)
  waiting for transfers between devices: 21.4 us -> 19.4 us
  starting transfers between devices: 32.8 us -> 33.7 us
    ppermute x21, waiting for transfers between devices: 21.4 us -> 19.4 us  [moved(): value = lax.ppermute(value, ('blk', 'rep'), pairs)]
    ppermute x21, starting transfers between devices: 32.8 us -> 33.7 us  [moved(): value = lax.ppermute(value, ('blk', 'rep'), pairs)]
  transfers between devices with their start and end apart: 21 -> 21, of which waited for: 7 -> 6; matrix products, arithmetic and copies ran while one was open for 1% -> 1% of each run, Pallas kernels for 27% -> 28%
where the time goes in v1:
time: 80.5 us; the launch traced here: 80.4 us
  starting transfers between devices  33.7 us (42%)
  Pallas kernels  26.3 us (33%)
  waiting for transfers between devices  19.4 us (24%)
    ppermute x21, starting transfers between devices, moved(): value = lax.ppermute(value, ('blk', 'rep'), pairs)  33.7 us
    ppermute x21, waiting for transfers between devices, moved(): value = lax.ppermute(value, ('blk', 'rep'), pairs)  19.4 us
    pallas_call x6, Pallas kernels, gathered(): pl.pallas_call(functools.partial(gather_kernel, chunks, offset, total is...  14.1 us
    pallas_call x1, Pallas kernels, load(): pl.pallas_call(functools.partial(load_kernel, parts), in_specs=[scalars]...  6.61 us
    pallas_call x1, Pallas kernels, degree(): pl.pallas_call(degree_kernel, in_specs=[pl.BlockSpec(memory_space=pltpu.S...  3.79 us
  transfers between devices with their start and end apart: 21, of which 6 were waited for; matrix products, arithmetic and copies ran while one was open for 1% of the time, Pallas kernels for 28%

profile of v1, /device:TPU:1, one launch (start us, length us, event | category | flops | bytes accessed | tf_op | source)
XLA Modules:
  0.0 80.4 jit_solution(4069626531740058621)
XLA Ops:
  0.0 1.2 %start.1 = (bf16[512,256]{1,0:T(8,128)(2,1)S(1)}, bf16[4,256,256]{2,1,0:T(8,128)(2,1)S(1)}) custom-call(s32[1]{0:T(128)} %bitcast.side_ref, bf16[512,256]{1,0:T(8,128)(2,1)} %codes_hbm.1, f32[2,512]{1,0:T(2,128)} %bitcast.7, bf16[1024,512]{1,0:T(8,128)(2,1)} %weight_hbm.1), custom_call_target="tpu_custom_call" | custom-call | tf_op jit(solution)/shard_map/start/pallas_call | solution.py:150
  1.2 2.5 %collective-permute-start = (bf16[512,256]{1,0:T(8,128)(2,1)S(1)}, bf16[512,256]{1,0:T(8,128)(2,1)S(1)}, u32[]{:S(2)}, u32[]{:S(2)}) collective-permute-start(bf16[512,256]{1,0:T(8,128)(2,1)S(1)} %get-tuple-element.15.features_ref), channel_id=1, source_target_pairs={{0,1},{1,0},{2,3},{3,2},{4,5},{5,4},{6,7},{7,6},{8,9},{9,8},{10,11... | collective-permute-start | bytes 786440 | tf_op jit(solution)/shard_map/ppermute | solution.py:57
  3.8 6.6 %load.1 = (bf16[513,128,128]{2,1,0:T(8,128)(2,1)S(1)}, s32[1024]{0:T(1024)S(1)}) custom-call(s32[1]{0:T(128)} %bitcast.2.device_ref, s32[128,2,128]{2,1,0:T(2,128)} %constant.12.clone.spots_hbm, s32[512]{0:T(512)} %source_hbm.1, s32[512]{0:T(512)} %target_ref.1, bf16[512,128,128]{2,1,0:T(8,128)(2,1)} %adjacency_hbm.1), custom_call_target="tpu_custom_call" | custom-call | flops 8388608 | bytes 16777216 | tf_op jit(solution)/shard_map/load/pallas_call | solution.py:278
  10.4 0.0 collective-permute-done.across_ref
  10.4 0.3 mix.2
  10.7 1.4 %collective-permute-start.1 = (bf16[512,256]{1,0:T(8,128)(2,1)S(1)}, bf16[512,256]{1,0:T(8,128)(2,1)S(1)}, u32[]{:S(2)}, u32[]{:S(2)}) collective-permute-start(bf16[512,256]{1,0:T(8,128)(2,1)S(1)} %mix.2), channel_id=1, source_target_pairs={{0,4},{1,5},{2,34},{3,35},{4,8},{5,9},{6,38},{7,39},{8,12},{9,13},... | collective-permute-start | bytes 786440 | tf_op jit(solution)/shard_map/ppermute | solution.py:57
  12.1 1.5 %collective-permute-start.2 = (bf16[512,256]{1,0:T(8,128)(2,1)S(1)}, bf16[512,256]{1,0:T(8,128)(2,1)S(1)}, u32[]{:S(2)}, u32[]{:S(2)}) collective-permute-start(bf16[512,256]{1,0:T(8,128)(2,1)S(1)} %mix.2), channel_id=1, source_target_pairs={{0,12},{1,13},{2,98},{3,99},{4,0},{5,1},{6,102},{7,103},{8,4},{9,5... | collective-permute-start | bytes 786440 | tf_op jit(solution)/shard_map/ppermute | solution.py:57
  13.6 1.6 %collective-permute-start.4 = (bf16[512,256]{1,0:T(8,128)(2,1)S(1)}, bf16[512,256]{1,0:T(8,128)(2,1)S(1)}, u32[]{:S(2)}, u32[]{:S(2)}) collective-permute-start(bf16[512,256]{1,0:T(8,128)(2,1)S(1)} %mix.2), channel_id=1, source_target_pairs={{0,8},{1,9},{2,66},{3,67},{4,12},{5,13},{6,70},{7,71},{8,0},{9,1},... | collective-permute-start | bytes 786440 | tf_op jit(solution)/shard_map/ppermute | solution.py:57
  15.2 3.4 %collective-permute-start.5 = (bf16[512,256]{1,0:T(8,128)(2,1)S(1)}, bf16[512,256]{1,0:T(8,128)(2,1)S(1)}, u32[]{:S(2)}, u32[]{:S(2)}) collective-permute-start(bf16[512,256]{1,0:T(8,128)(2,1)S(1)} %mix.2), channel_id=1, source_target_pairs={{0,16},{1,17},{2,18},{3,19},{4,20},{5,21},{6,22},{7,23},{8,24},{9,... | collective-permute-start | bytes 786440 | tf_op jit(solution)/shard_map/ppermute | solution.py:57
  18.5 0.0 collective-permute-done.1
  18.6 0.0 copy-start
  18.6 1.1 %collective-permute-done.2 = bf16[512,256]{1,0:T(8,128)(2,1)S(1)} collective-permute-done((bf16[512,256]{1,0:T(8,128)(2,1)S(1)}, bf16[512,256]{1,0:T(8,128)(2,1)S(1)}, u32[]{:S(2)}, u32[]{:S(2)}) %collective-permute-start.2) | collective-permute-done | bytes 262176 | tf_op jit(solution)/shard_map/ppermute | solution.py:57
  19.7 1.8 %collective-permute-done.4 = bf16[512,256]{1,0:T(8,128)(2,1)S(1)} collective-permute-done((bf16[512,256]{1,0:T(8,128)(2,1)S(1)}, bf16[512,256]{1,0:T(8,128)(2,1)S(1)}, u32[]{:S(2)}, u32[]{:S(2)}) %collective-permute-start.4) | collective-permute-done | bytes 262176 | tf_op jit(solution)/shard_map/ppermute | solution.py:57
  21.6 2.0 %collective-permute-done.5 = bf16[512,256]{1,0:T(8,128)(2,1)S(1)} collective-permute-done((bf16[512,256]{1,0:T(8,128)(2,1)S(1)}, bf16[512,256]{1,0:T(8,128)(2,1)S(1)}, u32[]{:S(2)}, u32[]{:S(2)}) %collective-permute-start.5) | collective-permute-done | bytes 262176 | tf_op jit(solution)/shard_map/ppermute | solution.py:57
  23.6 4.2 %collective-permute-start.8 = (bf16[2560,256]{1,0:T(8,128)(2,1)S(1)}, bf16[2560,256]{1,0:T(8,128)(2,1)S(1)}, u32[]{:S(2)}, u32[]{:S(2)}) collective-permute-start(bf16[2560,256]{1,0:T(8,128)(2,1)S(1)} %constant_dynamic-update-slice_fusion.refs_0_), channel_id=1, source_target_pairs={{0,96},{1,97},{2,14},{3,15},{4,100},{5,101},{6,2},{7,3},{8,104},{9... | collective-permute-start | bytes 3932168 | tf_op jit(solution)/shard_map/ppermute | solution.py:57
  27.8 0.0 collective-permute-start.6
  27.8 2.8 %collective-permute-start.3 = (bf16[1024,256]{1,0:T(8,128)(2,1)S(1)}, bf16[1024,256]{1,0:T(8,128)(2,1)S(1)}, u32[]{:S(2)}, u32[]{:S(2)}) collective-permute-start(bf16[1024,256]{1,0:T(8,128)(2,1)S(1)} %pad_maximum_fusion.2), channel_id=1, source_target_pairs={{0,16},{1,17},{2,18},{3,19},{4,20},{5,21},{6,22},{7,23},{8,24},{9,... | collective-permute-start | bytes 1572872 | tf_op jit(solution)/shard_map/ppermute | solution.py:57
  30.7 0.9 %collective-permute-start.18 = (bf16[2560,256]{1,0:T(8,128)(2,1)S(1)}, bf16[2560,256]{1,0:T(8,128)(2,1)S(1)}, u32[]{:S(2)}, u32[]{:S(2)}) collective-permute-start(bf16[2560,256]{1,0:T(8,128)(2,1)S(1)} %constant_dynamic-update-slice_fusion.refs_0_), channel_id=1, source_target_pairs={{0,2},{1,3},{2,0},{3,1},{4,6},{5,7},{6,4},{7,5},{8,10},{9,11},{10,... | collective-permute-start | bytes 3932168 | tf_op jit(solution)/shard_map/ppermute | solution.py:57
  31.6 0.0 copy-done
  31.6 0.0 copy-start.1
  31.6 3.8 %degree.1 = f32[4,128,128]{2,1,0:T(8,128)S(1)} custom-call(s32[512]{0:T(512)S(1)} %copy-done, bf16[513,128,128]{2,1,0:T(8,128)(2,1)S(1)} %get-tuple-element.18.tiles_ref), custom_call_target="tpu_custom_call" | custom-call | flops 8388608 | bytes 16777216 | tf_op jit(solution)/shard_map/degree/pallas_call | solution.py:252
  35.4 0.0 copy-done.1
  35.4 0.3 mix.3.refs_4_
  35.7 6.7 %collective-permute-done.8.refs_1_ = bf16[2560,256]{1,0:T(8,128)(2,1)S(1)} collective-permute-done((bf16[2560,256]{1,0:T(8,128)(2,1)S(1)}, bf16[2560,256]{1,0:T(8,128)(2,1)S(1)}, u32[]{:S(2)}, u32[]{:S(2)}) %collective-permute-start.8) | collective-permute-done | bytes 1310752 | tf_op jit(solution)/shard_map/ppermute | solution.py:57
  42.4 0.4 collective-permute-done.3.refs_0_
  42.8 0.1 pad_maximum_fusion
  42.9 3.1 %collective-permute-start.11 = (bf16[2432,256]{1,0:T(8,128)(2,1)S(1)}, bf16[2432,256]{1,0:T(8,128)(2,1)S(1)}, u32[]{:S(2)}, u32[]{:S(2)}) collective-permute-start(bf16[2432,256]{1,0:T(8,128)(2,1)S(1)} %pad_maximum_fusion), channel_id=1, source_target_pairs={{0,96},{1,97},{2,14},{3,15},{4,100},{5,101},{6,2},{7,3},{8,104},{9... | collective-permute-start | bytes 3735560 | tf_op jit(solution)/shard_map/ppermute | solution.py:57
  46.0 0.0 collective-permute-done.6.refs_0_
  46.0 0.1 pad_maximum_fusion.1
  46.1 0.1 collective-permute-start.7
  46.3 2.8 %collective-permute-start.9 = (bf16[1024,256]{1,0:T(8,128)(2,1)S(1)}, bf16[1024,256]{1,0:T(8,128)(2,1)S(1)}, u32[]{:S(2)}, u32[]{:S(2)}) collective-permute-start(bf16[1024,256]{1,0:T(8,128)(2,1)S(1)} %pad_maximum_fusion.3), channel_id=1, source_target_pairs={{0,16},{1,17},{2,18},{3,19},{4,20},{5,21},{6,22},{7,23},{8,24},{9,... | collective-permute-start | bytes 1572872 | tf_op jit(solution)/shard_map/ppermute | solution.py:57
  49.1 1.7 %collective-permute-start.16 = (bf16[2560,256]{1,0:T(8,128)(2,1)S(1)}, bf16[2560,256]{1,0:T(8,128)(2,1)S(1)}, u32[]{:S(2)}, u32[]{:S(2)}) collective-permute-start(bf16[2560,256]{1,0:T(8,128)(2,1)S(1)} %collective-permute-done.6.refs_0_), channel_id=1, source_target_pairs={{0,2},{1,3},{2,0},{3,1},{4,6},{5,7},{6,4},{7,5},{8,10},{9,11},{10,... | collective-permute-start | bytes 3932168 | tf_op jit(solution)/shard_map/ppermute | solution.py:57
  50.8 0.0 collective-permute-done.18.refs_1_
  50.8 0.0 collective-permute-start.17
  50.9 2.1 %gather.6.refs_4_ = f32[512,256]{1,0:T(8,128)S(1)} custom-call(s32[1024]{0:T(1024)S(1)} %get-tuple-element.19.table_ref, bf16[513,128,128]{2,1,0:T(8,128)(2,1)S(1)} %get-tuple-element.18.tiles_ref, bf16[2560,256]{1,0:T(8,128)(2,1)S(1)} %constant_dynamic-update-slice_fusion.refs_0_, bf16[2560,256]{1,0:T(8,128)(2,1)S(1)} %collective-permute-done.18.refs_1_), custom_call_target="tpu_custom_call" | custom-call | flops 26843545600 | bytes 3932160 | tf_op jit(solution)/shard_map/gather/pallas_call | solution.py:351
  53.0 7.4 %collective-permute-done.9.refs_2_ = bf16[1024,256]{1,0:T(8,128)(2,1)S(1)} collective-permute-done((bf16[1024,256]{1,0:T(8,128)(2,1)S(1)}, bf16[1024,256]{1,0:T(8,128)(2,1)S(1)}, u32[]{:S(2)}, u32[]{:S(2)}) %collective-permute-start.9) | collective-permute-done | bytes 524320 | tf_op jit(solution)/shard_map/ppermute | solution.py:57
  60.3 1.9 %collective-permute-start.20 = (bf16[1024,256]{1,0:T(8,128)(2,1)S(1)}, bf16[1024,256]{1,0:T(8,128)(2,1)S(1)}, u32[]{:S(2)}, u32[]{:S(2)}) collective-permute-start(bf16[1024,256]{1,0:T(8,128)(2,1)S(1)} %collective-permute-done.3.refs_0_), channel_id=1, source_target_pairs={{0,2},{1,3},{2,0},{3,1},{4,6},{5,7},{6,4},{7,5},{8,10},{9,11},{10,... | collective-permute-start | bytes 1572872 | tf_op jit(solution)/shard_map/ppermute | solution.py:57
  62.2 0.0 collective-permute-done.7.refs_0_
  62.3 0.1 collective-permute-start.10
  62.4 0.0 collective-permute-done.11.refs_1_
  62.4 1.7 %collective-permute-start.14 = (bf16[2176,256]{1,0:T(8,128)(2,1)S(1)}, bf16[2176,256]{1,0:T(8,128)(2,1)S(1)}, u32[]{:S(2)}, u32[]{:S(2)}) collective-permute-start(bf16[2176,256]{1,0:T(8,128)(2,1)S(1)} %collective-permute-done.7.refs_0_), channel_id=1, source_target_pairs={{0,2},{1,3},{2,0},{3,1},{4,6},{5,7},{6,4},{7,5},{8,10},{9,11},{10,... | collective-permute-start | bytes 3342344 | tf_op jit(solution)/shard_map/ppermute | solution.py:57
  64.2 0.0 collective-permute-done.16.refs_2_
  64.2 1.6 %collective-permute-start.12 = (bf16[1024,256]{1,0:T(8,128)(2,1)S(1)}, bf16[1024,256]{1,0:T(8,128)(2,1)S(1)}, u32[]{:S(2)}, u32[]{:S(2)}) collective-permute-start(bf16[1024,256]{1,0:T(8,128)(2,1)S(1)} %pad_maximum_fusion.5), channel_id=1, source_target_pairs={{0,96},{1,97},{2,14},{3,15},{4,100},{5,101},{6,2},{7,3},{8,104},{9... | collective-permute-start | bytes 1572872 | tf_op jit(solution)/shard_map/ppermute | solution.py:57
  65.8 0.0 collective-permute-done.17.refs_3_
  65.8 1.6 %collective-permute-start.15 = (bf16[2432,256]{1,0:T(8,128)(2,1)S(1)}, bf16[2432,256]{1,0:T(8,128)(2,1)S(1)}, u32[]{:S(2)}, u32[]{:S(2)}) collective-permute-start(bf16[2432,256]{1,0:T(8,128)(2,1)S(1)} %collective-permute-done.11.refs_1_), channel_id=1, source_target_pairs={{0,2},{1,3},{2,0},{3,1},{4,6},{5,7},{6,4},{7,5},{8,10},{9,11},{10,... | collective-permute-start | bytes 3735560 | tf_op jit(solution)/shard_map/ppermute | solution.py:57
  67.4 3.5 %gather.7.refs_2_ = f32[512,256]{1,0:T(8,128)S(1)} custom-call(s32[1024]{0:T(1024)S(1)} %get-tuple-element.19.table_ref, bf16[513,128,128]{2,1,0:T(8,128)(2,1)S(1)} %get-tuple-element.18.tiles_ref, bf16[2560,256]{1,0:T(8,128)(2,1)S(1)} %collective-permute-done.6.refs_0_, bf16[2560,256]{1,0:T(8,128)(2,1)S(1)} %collective-permute-done.8.refs_1_, ...), custom_call_target="tpu_custom_call" | custom-call | flops 53687091200 | bytes 7864320 | tf_op jit(solution)/shard_map/gather/pallas_call | solution.py:351
  70.9 0.0 collective-permute-done.20.refs_1_
  70.9 0.3 collective-permute-start.19
  71.2 1.3 %gather.8.refs_3_ = f32[512,256]{1,0:T(8,128)S(1)} custom-call(s32[1024]{0:T(1024)S(1)} %get-tuple-element.19.table_ref, bf16[513,128,128]{2,1,0:T(8,128)(2,1)S(1)} %get-tuple-element.18.tiles_ref, bf16[1024,256]{1,0:T(8,128)(2,1)S(1)} %collective-permute-done.3.refs_0_, bf16[1024,256]{1,0:T(8,128)(2,1)S(1)} %collective-permute-done.20.refs_1_, ...), custom_call_target="tpu_custom_call" | custom-call | flops 10737418240 | bytes 1572864 | tf_op jit(solution)/shard_map/gather/pallas_call | solution.py:351
  72.5 2.3 %gather.9.refs_3_ = f32[512,256]{1,0:T(8,128)S(1)} custom-call(s32[1024]{0:T(1024)S(1)} %get-tuple-element.19.table_ref, bf16[513,128,128]{2,1,0:T(8,128)(2,1)S(1)} %get-tuple-element.18.tiles_ref, bf16[2176,256]{1,0:T(8,128)(2,1)S(1)} %collective-permute-done.7.refs_0_, bf16[2432,256]{1,0:T(8,128)(2,1)S(1)} %collective-permute-done.11.refs_1_, ...), custom_call_target="tpu_custom_call" | custom-call | flops 29527900160 | bytes 4325376 | tf_op jit(solution)/shard_map/gather/pallas_call | solution.py:351
  74.8 0.0 collective-permute-done.10
  74.9 0.0 collective-permute-done.12
  74.9 0.6 collective-permute-start.13
  75.5 0.0 collective-permute-done.19.refs_2_
  75.5 0.0 collective-permute-done.14.refs_0_
  75.5 0.0 collective-permute-done.15.refs_1_
  75.5 2.3 %gather.10.refs_2_ = f32[512,256]{1,0:T(8,128)S(1)} custom-call(s32[1024]{0:T(1024)S(1)} %get-tuple-element.19.table_ref, bf16[513,128,128]{2,1,0:T(8,128)(2,1)S(1)} %get-tuple-element.18.tiles_ref, bf16[2176,256]{1,0:T(8,128)(2,1)S(1)} %collective-permute-done.14.refs_0_, bf16[2432,256]{1,0:T(8,128)(2,1)S(1)} %collective-permute-done.15.refs_1_, ...), custom_call_target="tpu_custom_call" | custom-call | flops 29527900160 | bytes 4325376 | tf_op jit(solution)/shard_map/gather/pallas_call | solution.py:351
  77.8 0.0 collective-permute-done.13.refs_1_
  77.8 2.6 %gather.11 = bf16[512,256]{1,0:T(8,128)(2,1)} custom-call(s32[1024]{0:T(1024)S(1)} %get-tuple-element.19.table_ref, bf16[513,128,128]{2,1,0:T(8,128)(2,1)S(1)} %get-tuple-element.18.tiles_ref, bf16[2048,256]{1,0:T(8,128)(2,1)S(1)} %constant_dynamic-update-slice_fusion.5.refs_0_, bf16[2048,256]{1,0:T(8,128)(2,1)S(1)} %collective-permute-done.13.refs_1_, ...), custom_call_target="tpu_custom_call" | custom-call | flops 21474836480 | bytes 3145728 | tf_op jit(solution)/shard_map/gather/pallas_call | solution.py:351
  (18 shorter events, 0.5 us)
Async XLA Ops:
  1.2 9.2 %collective-permute-start = (bf16[512,256]{1,0:T(8,128)(2,1)S(1)}, bf16[512,256]{1,0:T(8,128)(2,1)S(1)}, u32[]{:S(2)}, u32[]{:S(2)}) collective-permute-start(bf16[512,256]{1,0:T(8,128)(2,1)S(1)} %get-tuple-element.15.features_ref), channel_id=1, source_target_pairs={{0,1},{1,0},{2,3},{3,2},{4,5},{5,4},{6,7},{7,6},{8,9},{9,8},{10,11... | collective-permute-start | bytes 786440 | tf_op jit(solution)/shard_map/ppermute | solution.py:57
  10.7 7.8 %collective-permute-start.1 = (bf16[512,256]{1,0:T(8,128)(2,1)S(1)}, bf16[512,256]{1,0:T(8,128)(2,1)S(1)}, u32[]{:S(2)}, u32[]{:S(2)}) collective-permute-start(bf16[512,256]{1,0:T(8,128)(2,1)S(1)} %mix.2), channel_id=1, source_target_pairs={{0,4},{1,5},{2,34},{3,35},{4,8},{5,9},{6,38},{7,39},{8,12},{9,13},... | collective-permute-start | bytes 786440 | tf_op jit(solution)/shard_map/ppermute | solution.py:57
  12.1 7.6 %collective-permute-start.2 = (bf16[512,256]{1,0:T(8,128)(2,1)S(1)}, bf16[512,256]{1,0:T(8,128)(2,1)S(1)}, u32[]{:S(2)}, u32[]{:S(2)}) collective-permute-start(bf16[512,256]{1,0:T(8,128)(2,1)S(1)} %mix.2), channel_id=1, source_target_pairs={{0,12},{1,13},{2,98},{3,99},{4,0},{5,1},{6,102},{7,103},{8,4},{9,5... | collective-permute-start | bytes 786440 | tf_op jit(solution)/shard_map/ppermute | solution.py:57
  13.6 8.0 %collective-permute-start.4 = (bf16[512,256]{1,0:T(8,128)(2,1)S(1)}, bf16[512,256]{1,0:T(8,128)(2,1)S(1)}, u32[]{:S(2)}, u32[]{:S(2)}) collective-permute-start(bf16[512,256]{1,0:T(8,128)(2,1)S(1)} %mix.2), channel_id=1, source_target_pairs={{0,8},{1,9},{2,66},{3,67},{4,12},{5,13},{6,70},{7,71},{8,0},{9,1},... | collective-permute-start | bytes 786440 | tf_op jit(solution)/shard_map/ppermute | solution.py:57
  15.2 8.4 %collective-permute-start.5 = (bf16[512,256]{1,0:T(8,128)(2,1)S(1)}, bf16[512,256]{1,0:T(8,128)(2,1)S(1)}, u32[]{:S(2)}, u32[]{:S(2)}) collective-permute-start(bf16[512,256]{1,0:T(8,128)(2,1)S(1)} %mix.2), channel_id=1, source_target_pairs={{0,16},{1,17},{2,18},{3,19},{4,20},{5,21},{6,22},{7,23},{8,24},{9,... | collective-permute-start | bytes 786440 | tf_op jit(solution)/shard_map/ppermute | solution.py:57
  18.6 13.0 %copy-start = (s32[512]{0:T(512)S(1)}, s32[512]{0:T(512)}, u32[]{:S(2)}) copy-start(s32[512]{0:T(512)} %target_ref.1) | copy-start | bytes 6148
  23.6 18.8 %collective-permute-start.8 = (bf16[2560,256]{1,0:T(8,128)(2,1)S(1)}, bf16[2560,256]{1,0:T(8,128)(2,1)S(1)}, u32[]{:S(2)}, u32[]{:S(2)}) collective-permute-start(bf16[2560,256]{1,0:T(8,128)(2,1)S(1)} %constant_dynamic-update-slice_fusion.refs_0_), channel_id=1, source_target_pairs={{0,96},{1,97},{2,14},{3,15},{4,100},{5,101},{6,2},{7,3},{8,104},{9... | collective-permute-start | bytes 3932168 | tf_op jit(solution)/shard_map/ppermute | solution.py:57
  27.8 18.2 %collective-permute-start.6 = (bf16[2560,256]{1,0:T(8,128)(2,1)S(1)}, bf16[2560,256]{1,0:T(8,128)(2,1)S(1)}, u32[]{:S(2)}, u32[]{:S(2)}) collective-permute-start(bf16[2560,256]{1,0:T(8,128)(2,1)S(1)} %constant_dynamic-update-slice_fusion.refs_0_), channel_id=1, source_target_pairs={{0,32},{1,33},{2,6},{3,7},{4,36},{5,37},{6,10},{7,11},{8,40},{9,41... | collective-permute-start | bytes 3932168 | tf_op jit(solution)/shard_map/ppermute | solution.py:57
  27.8 15.0 %collective-permute-start.3 = (bf16[1024,256]{1,0:T(8,128)(2,1)S(1)}, bf16[1024,256]{1,0:T(8,128)(2,1)S(1)}, u32[]{:S(2)}, u32[]{:S(2)}) collective-permute-start(bf16[1024,256]{1,0:T(8,128)(2,1)S(1)} %pad_maximum_fusion.2), channel_id=1, source_target_pairs={{0,16},{1,17},{2,18},{3,19},{4,20},{5,21},{6,22},{7,23},{8,24},{9,... | collective-permute-start | bytes 1572872 | tf_op jit(solution)/shard_map/ppermute | solution.py:57
  30.7 20.2 %collective-permute-start.18 = (bf16[2560,256]{1,0:T(8,128)(2,1)S(1)}, bf16[2560,256]{1,0:T(8,128)(2,1)S(1)}, u32[]{:S(2)}, u32[]{:S(2)}) collective-permute-start(bf16[2560,256]{1,0:T(8,128)(2,1)S(1)} %constant_dynamic-update-slice_fusion.refs_0_), channel_id=1, source_target_pairs={{0,2},{1,3},{2,0},{3,1},{4,6},{5,7},{6,4},{7,5},{8,10},{9,11},{10,... | collective-permute-start | bytes 3932168 | tf_op jit(solution)/shard_map/ppermute | solution.py:57
  31.6 3.8 %copy-start.1 = (f32[256]{0:T(256)S(1)}, f32[256]{0:T(256)}, u32[]{:S(2)}) copy-start(f32[256]{0:T(256)} %param.14) | copy-start | bytes 3076
  42.9 19.5 %collective-permute-start.11 = (bf16[2432,256]{1,0:T(8,128)(2,1)S(1)}, bf16[2432,256]{1,0:T(8,128)(2,1)S(1)}, u32[]{:S(2)}, u32[]{:S(2)}) collective-permute-start(bf16[2432,256]{1,0:T(8,128)(2,1)S(1)} %pad_maximum_fusion), channel_id=1, source_target_pairs={{0,96},{1,97},{2,14},{3,15},{4,100},{5,101},{6,2},{7,3},{8,104},{9... | collective-permute-start | bytes 3735560 | tf_op jit(solution)/shard_map/ppermute | solution.py:57
  46.1 16.1 %collective-permute-start.7 = (bf16[2176,256]{1,0:T(8,128)(2,1)S(1)}, bf16[2176,256]{1,0:T(8,128)(2,1)S(1)}, u32[]{:S(2)}, u32[]{:S(2)}) collective-permute-start(bf16[2176,256]{1,0:T(8,128)(2,1)S(1)} %pad_maximum_fusion.1), channel_id=1, source_target_pairs={{0,32},{1,33},{2,6},{3,7},{4,36},{5,37},{6,10},{7,11},{8,40},{9,41... | collective-permute-start | bytes 3342344 | tf_op jit(solution)/shard_map/ppermute | solution.py:57
  46.3 14.0 %collective-permute-start.9 = (bf16[1024,256]{1,0:T(8,128)(2,1)S(1)}, bf16[1024,256]{1,0:T(8,128)(2,1)S(1)}, u32[]{:S(2)}, u32[]{:S(2)}) collective-permute-start(bf16[1024,256]{1,0:T(8,128)(2,1)S(1)} %pad_maximum_fusion.3), channel_id=1, source_target_pairs={{0,16},{1,17},{2,18},{3,19},{4,20},{5,21},{6,22},{7,23},{8,24},{9,... | collective-permute-start | bytes 1572872 | tf_op jit(solution)/shard_map/ppermute | solution.py:57
  49.1 15.0 %collective-permute-start.16 = (bf16[2560,256]{1,0:T(8,128)(2,1)S(1)}, bf16[2560,256]{1,0:T(8,128)(2,1)S(1)}, u32[]{:S(2)}, u32[]{:S(2)}) collective-permute-start(bf16[2560,256]{1,0:T(8,128)(2,1)S(1)} %collective-permute-done.6.refs_0_), channel_id=1, source_target_pairs={{0,2},{1,3},{2,0},{3,1},{4,6},{5,7},{6,4},{7,5},{8,10},{9,11},{10,... | collective-permute-start | bytes 3932168 | tf_op jit(solution)/shard_map/ppermute | solution.py:57
  50.8 14.9 %collective-permute-start.17 = (bf16[2560,256]{1,0:T(8,128)(2,1)S(1)}, bf16[2560,256]{1,0:T(8,128)(2,1)S(1)}, u32[]{:S(2)}, u32[]{:S(2)}) collective-permute-start(bf16[2560,256]{1,0:T(8,128)(2,1)S(1)} %collective-permute-done.8.refs_1_), channel_id=1, source_target_pairs={{0,2},{1,3},{2,0},{3,1},{4,6},{5,7},{6,4},{7,5},{8,10},{9,11},{10,... | collective-permute-start | bytes 3932168 | tf_op jit(solution)/shard_map/ppermute | solution.py:57
  60.3 10.5 %collective-permute-start.20 = (bf16[1024,256]{1,0:T(8,128)(2,1)S(1)}, bf16[1024,256]{1,0:T(8,128)(2,1)S(1)}, u32[]{:S(2)}, u32[]{:S(2)}) collective-permute-start(bf16[1024,256]{1,0:T(8,128)(2,1)S(1)} %collective-permute-done.3.refs_0_), channel_id=1, source_target_pairs={{0,2},{1,3},{2,0},{3,1},{4,6},{5,7},{6,4},{7,5},{8,10},{9,11},{10,... | collective-permute-start | bytes 1572872 | tf_op jit(solution)/shard_map/ppermute | solution.py:57
  62.3 12.5 %collective-permute-start.10 = (bf16[1024,256]{1,0:T(8,128)(2,1)S(1)}, bf16[1024,256]{1,0:T(8,128)(2,1)S(1)}, u32[]{:S(2)}, u32[]{:S(2)}) collective-permute-start(bf16[1024,256]{1,0:T(8,128)(2,1)S(1)} %pad_maximum_fusion.4), channel_id=1, source_target_pairs={{0,32},{1,33},{2,6},{3,7},{4,36},{5,37},{6,10},{7,11},{8,40},{9,41... | collective-permute-start | bytes 1572872 | tf_op jit(solution)/shard_map/ppermute | solution.py:57
  62.4 13.1 %collective-permute-start.14 = (bf16[2176,256]{1,0:T(8,128)(2,1)S(1)}, bf16[2176,256]{1,0:T(8,128)(2,1)S(1)}, u32[]{:S(2)}, u32[]{:S(2)}) collective-permute-start(bf16[2176,256]{1,0:T(8,128)(2,1)S(1)} %collective-permute-done.7.refs_0_), channel_id=1, source_target_pairs={{0,2},{1,3},{2,0},{3,1},{4,6},{5,7},{6,4},{7,5},{8,10},{9,11},{10,... | collective-permute-start | bytes 3342344 | tf_op jit(solution)/shard_map/ppermute | solution.py:57
  64.2 10.7 %collective-permute-start.12 = (bf16[1024,256]{1,0:T(8,128)(2,1)S(1)}, bf16[1024,256]{1,0:T(8,128)(2,1)S(1)}, u32[]{:S(2)}, u32[]{:S(2)}) collective-permute-start(bf16[1024,256]{1,0:T(8,128)(2,1)S(1)} %pad_maximum_fusion.5), channel_id=1, source_target_pairs={{0,96},{1,97},{2,14},{3,15},{4,100},{5,101},{6,2},{7,3},{8,104},{9... | collective-permute-start | bytes 1572872 | tf_op jit(solution)/shard_map/ppermute | solution.py:57
  65.8 9.7 %collective-permute-start.15 = (bf16[2432,256]{1,0:T(8,128)(2,1)S(1)}, bf16[2432,256]{1,0:T(8,128)(2,1)S(1)}, u32[]{:S(2)}, u32[]{:S(2)}) collective-permute-start(bf16[2432,256]{1,0:T(8,128)(2,1)S(1)} %collective-permute-done.11.refs_1_), channel_id=1, source_target_pairs={{0,2},{1,3},{2,0},{3,1},{4,6},{5,7},{6,4},{7,5},{8,10},{9,11},{10,... | collective-permute-start | bytes 3735560 | tf_op jit(solution)/shard_map/ppermute | solution.py:57
  70.9 4.6 %collective-permute-start.19 = (bf16[1024,256]{1,0:T(8,128)(2,1)S(1)}, bf16[1024,256]{1,0:T(8,128)(2,1)S(1)}, u32[]{:S(2)}, u32[]{:S(2)}) collective-permute-start(bf16[1024,256]{1,0:T(8,128)(2,1)S(1)} %collective-permute-done.9.refs_2_), channel_id=1, source_target_pairs={{0,2},{1,3},{2,0},{3,1},{4,6},{5,7},{6,4},{7,5},{8,10},{9,11},{10,... | collective-permute-start | bytes 1572872 | tf_op jit(solution)/shard_map/ppermute | solution.py:57
  74.9 2.9 %collective-permute-start.13 = (bf16[2048,256]{1,0:T(8,128)(2,1)S(1)}, bf16[2048,256]{1,0:T(8,128)(2,1)S(1)}, u32[]{:S(2)}, u32[]{:S(2)}) collective-permute-start(bf16[2048,256]{1,0:T(8,128)(2,1)S(1)} %constant_dynamic-update-slice_fusion.5.refs_0_), channel_id=1, source_target_pairs={{0,2},{1,3},{2,0},{3,1},{4,6},{5,7},{6,4},{7,5},{8,10},{9,11},{10,... | collective-permute-start | bytes 3145736 | tf_op jit(solution)/shard_map/ppermute | solution.py:57
